TPU v7x, 32 devices: a whole 2x2x4 slice. The times are simulated.
32 devices in a mesh: lon: 16 (over z, y, core), lat: 2 (over x).
Axes of the slice: x: 2, y: 2, z: 4, core: 2. Of those that a mesh axis runs over, the one named last changes fastest.
Arguments:
- field: float32 [2, 12, 1280, 640], P(None, 'lat', 'lon'), may hold values from -6 to 6
- spectral_filter: float32 [2, 7, 640, 640], P(None, None, None, 'lon'), may hold values from -2 to 2
- w_in: bfloat16 [640, 1280], replicated, may hold values from -0.25 to 0.25
- w_out: bfloat16 [1280, 640], replicated, may hold values from -0.15625 to 0.15625
Outputs:
- result: float32 [2, 12, 1280, 640], P(None, 'lat', 'lon')
All inputs are finite; a program needn't handle non-finite values.
Results may differ from a plain program's by a relative error of at most 0.0016.
Values sent between devices are 32-bit elements; how exact they have to be, the bound alone decides.
A program may use at most 64 MiB of HBM per device.

v0:
```python
import jax
import jax.numpy as jnp
from jax import lax
from jax.sharding import PartitionSpec as P


def shifted(block, axis, distance):
    devices = range(lax.axis_size(axis))
    route = [(i - distance, i) for i in devices if i - distance in devices]
    return lax.ppermute(block, axis, route)


def forward_table(length, modes):
    places = jnp.arange(length, dtype=jnp.int32)[:, None]
    orders = jnp.arange(modes, dtype=jnp.int32)[None, :]
    angles = 2.0 * jnp.pi / length * (places * orders % length).astype(jnp.float32)
    return jnp.concatenate([jnp.cos(angles), -jnp.sin(angles)], axis=1)


def inverse_table(length, modes):
    orders = jnp.arange(modes, dtype=jnp.int32)[:, None]
    places = jnp.arange(length, dtype=jnp.int32)[None, :]
    angles = 2.0 * jnp.pi / length * (places * orders % length).astype(jnp.float32)
    weights = jnp.where(orders == 0, jnp.float32(1.0), jnp.float32(2.0)) / length
    return jnp.concatenate([weights * jnp.cos(angles), -weights * jnp.sin(angles)], axis=0)


def swapped_halves(spectrum, modes):
    return jnp.concatenate([spectrum[..., modes:], spectrum[..., :modes]], axis=3)


def body(field, spectral_filter, w_in, w_out):
    members, lat_rows, lon_local, channels = field.shape
    groups = lax.axis_size("lon")
    lon_total = lon_local * groups
    modes = lon_total // 2
    table_fwd = forward_table(lon_total, modes)
    table_inv = inverse_table(lon_total, modes)
    gridded = lax.all_to_all(field, "lon", split_axis=3, concat_axis=2, tiled=True)
    spectrum = jnp.einsum("eilc,lk->eick", gridded, table_fwd, precision=lax.Precision.HIGHEST)
    filt_real = jnp.transpose(spectral_filter[0], (0, 2, 1))
    filt_imag = jnp.transpose(spectral_filter[1], (0, 2, 1))
    coef_same = jnp.concatenate([filt_real, filt_real], axis=2)
    coef_cross = jnp.concatenate([-filt_imag, filt_imag], axis=2)

    def tap_term(offset, values, crossed):
        return coef_same[offset][None, None] * values + coef_cross[offset][None, None] * crossed

    padded = jnp.pad(spectrum, ((0, 0), (6, 6), (0, 0), (0, 0)))
    crossed = swapped_halves(padded, modes)
    span = lat_rows + 6
    extended = tap_term(0, padded[:, 0:span], crossed[:, 0:span])
    for offset in range(1, 7):
        extended = extended + tap_term(
            offset, padded[:, offset : offset + span], crossed[:, offset : offset + span]
        )
    upper = extended[:, :3]
    lower = extended[:, lat_rows + 3 :]
    from_below = shifted(upper, "lat", -1)
    from_above = shifted(lower, "lat", 1)
    convolved = extended[:, 3 : lat_rows + 3]
    convolved = convolved.at[:, :3].add(from_above)
    convolved = convolved.at[:, lat_rows - 3 :].add(from_below)
    grid_out = jnp.einsum("eick,kl->eicl", convolved, table_inv, precision=lax.Precision.HIGHEST)
    returned = lax.all_to_all(grid_out, "lon", split_axis=3, concat_axis=2, tiled=True)
    mixed = field + jnp.transpose(returned, (0, 1, 3, 2))
    rows = mixed.reshape(-1, channels)
    center = jnp.mean(rows, axis=1, keepdims=True)
    spread = jnp.mean((rows - center) ** 2, axis=1, keepdims=True)
    normed = ((rows - center) / jnp.sqrt(spread + 1e-05)).astype(jnp.bfloat16)
    before = jnp.dot(normed, w_in, preferred_element_type=jnp.float32)
    hidden = jax.nn.gelu(before, approximate=False).astype(jnp.bfloat16)
    update = jnp.dot(hidden, w_out, preferred_element_type=jnp.float32)
    return mixed + update.reshape(mixed.shape)


def solution(mesh):
    in_specs = (P(None, "lat", "lon", None), P(None, None, None, "lon"), P(), P())
    out_specs = P(None, "lat", "lon", None)
    return jax.shard_map(body, mesh=mesh, in_specs=in_specs, out_specs=out_specs, check_vma=False)
```

profile of v0, /device:TPU:1, one launch (start us, length us, event | category | flops | bytes accessed | tf_op | source)
XLA Modules:
  0.0 336.9 jit_solution(7720879087108914878)
XLA Ops:
  0.0 0.0 copy-start
  0.0 6.0 %copy.38 = f32[2,6,80,640]{2,0,1,3:T(2,128)} copy(f32[2,6,80,640]{3,2,1,0:T(8,128)} %param.8) | data formatting | bytes 4915200 | tf_op args[0]
  6.0 0.0 copy-start.1
  6.0 7.5 %all-to-all-start = ((f32[2,6,80,640]{2,0,1,3:T(2,128)}), f32[2,6,80,640]{2,0,1,3:T(2,128)}, u32[]{:S(2)}, u32[]{:S(2)}) async-start(f32[2,6,80,640]{2,0,1,3:T(2,128)} %copy.38), calls=%async_computation | async-start | bytes 7864320 | tf_op jit(solution)/shard_map/all_to_all | solution.py:39
  13.5 0.0 copy-done.1
  13.5 0.1 slice_bitcast_fusion.1
  13.6 0.1 fusion.82
  13.8 1.0 fusion.70
  14.7 14.5 %sine_negate_fusion = (f32[1280,640]{1,0:T(8,128)}, f32[1280,640]{1,0:T(8,128)}) fusion(), kind=kLoop, calls=%fused_computation.93 | loop fusion | flops 8192000 | bytes 6553600 | tf_op jit(solution)/shard_map/neg | solution.py:17
  29.3 57.7 %all-to-all-done = f32[2,6,80,640]{2,0,1,3:T(2,128)} async-done(((f32[2,6,80,640]{2,0,1,3:T(2,128)}), f32[2,6,80,640]{2,0,1,3:T(2,128)}, u32[]{:S(2)}, u32[]{:S(2)}) %all-to-all-start) | async-done | bytes 2457632 | tf_op jit(solution)/shard_map/all_to_all | solution.py:39
  87.0 2.4 copy.39
  89.5 2.5 copy.40
  92.0 5.3 %all_to_all.29 = f32[2,6,1280,40]{2,3,1,0:T(8,128)} reshape(f32[2,6,16,80,40]{3,2,4,1,0:T(8,128)} %copy.40) | data formatting | bytes 4915200 | tf_op jit(solution)/shard_map/all_to_all | solution.py:39
  97.4 14.5 %fusion.60 = f32[2,6,40,1280]{3,2,1,0:T(8,128)S(1)} fusion(f32[2,6,1280,40]{2,3,1,0:T(8,128)} %all_to_all.29, f32[1280,640]{1,0:T(8,128)} %get-tuple-element.51, f32[1280,640]{1,0:T(8,128)} %get-tuple-element.52), kind=kOutput, calls=%fused_computation.100 | convolution fusion | flops 9438822400 | bytes 11468800 | tf_op jit(solution)/shard_map/eilc,lk->eick/dot_general | solution.py:40
  111.8 0.0 copy-start.2
  111.8 0.0 copy-start.3
  111.8 0.0 copy-start.4
  111.8 0.0 copy-start.5
  111.9 0.0 copy-start.6
  111.9 0.5 pad_slice_fusion.6
  112.4 0.4 copy-done.2
  112.8 0.1 copy-done.3
  112.9 0.1 copy-done.4
  113.0 0.1 copy-done.5
  113.1 0.1 copy-done.6
  113.1 5.1 %fusion.13 = f32[2,12,40,1280]{3,2,1,0:T(8,128)S(1)} fusion(f32[2,18,40,640]{3,2,1,0:T(8,128)S(1)} %get-tuple-element.34, f32[2,18,40,640]{3,2,1,0:T(8,128)S(1)} %get-tuple-element.33, f32[2,6,40,1280]{3,2,1,0:T(8,128)S(1)} %fusion.60, f32[40,1280]{1,0:T(8,128)S(1)} %copy-done.5, f32[40,1280]{1,0:T(8,128)S(1)} %get-tuple-element.48, ...), kind=kLoop, calls=%fused_computation.37 | loop fusion | flops 41779200 | bytes 17612800 | tf_op jit(solution)/shard_map/add | solution.py:54
  118.2 0.2 fusion.128
  118.4 3.2 collective-permute-start
  121.6 1.5 collective-permute-start.1
  123.1 14.1 %sine_multiply_fusion = (f32[640,1280]{1,0:T(8,128)S(1)}, f32[640,1280]{1,0:T(8,128)S(1)}) fusion(f32[640]{0:T(1024)S(1)} %fusion.93, f32[640]{0:T(1024)S(1)} %select_multiply_fusion), kind=kLoop, calls=%fused_computation.88 | loop fusion | flops 9011200 | bytes 6558720 | tf_op jit(solution)/shard_map/mul | solution.py:25
  137.3 0.2 slice.237
  137.5 10.7 %collective-permute-done = f32[2,3,40,1280]{3,2,1,0:T(8,128)S(1)} collective-permute-done((f32[2,3,40,1280]{3,2,1,0:T(8,128)S(1)}, f32[2,3,40,1280]{3,2,1,0:T(8,128)S(1)}, u32[]{:S(2)}, u32[]{:S(2)}) %collective-permute-start) | collective-permute-done | bytes 1228832 | tf_op jit(solution)/shard_map/ppermute | solution.py:10
  148.1 0.2 fusion.66
  148.3 3.8 %collective-permute-done.1 = f32[2,3,40,1280]{3,2,1,0:T(8,128)S(1)} collective-permute-done((f32[2,3,40,1280]{3,2,1,0:T(8,128)S(1)}, f32[2,3,40,1280]{3,2,1,0:T(8,128)S(1)}, u32[]{:S(2)}, u32[]{:S(2)}) %collective-permute-start.1) | collective-permute-done | bytes 1228832 | tf_op jit(solution)/shard_map/ppermute | solution.py:10
  152.2 0.3 fusion.65
  152.4 11.5 %fusion.3 = f32[2,6,40,1280]{3,2,1,0:T(8,128)} fusion(f32[2,6,40,1280]{3,2,1,0:T(8,128)S(1)} %fusion.65, f32[640,1280]{1,0:T(8,128)S(1)} %get-tuple-element.53, f32[640,1280]{1,0:T(8,128)S(1)} %get-tuple-element.54), kind=kOutput, calls=%fused_computation.27 | convolution fusion | flops 9438822400 | bytes 11468800 | tf_op jit(solution)/shard_map/eick,kl->eicl/dot_general | solution.py:64
  164.0 9.9 %copy.41 = f32[2,6,40,1280]{2,0,1,3:T(2,128)} copy(f32[2,6,40,1280]{3,2,1,0:T(8,128)} %fusion.3) | data formatting | bytes 4915200 | tf_op jit(solution)/shard_map/eick,kl->eicl/dot_general | solution.py:64
  173.9 16.8 %reshape.138 = f32[16,1,38400]{2,1,0:T(1,128)} reshape(f32[1280,6,2,40]{3,2,1,0:T(2,128)} %bitcast.80) | data formatting | bytes 4915200
  190.7 75.2 %all_to_all.36 = f32[16,1,38400]{2,1,0:T(1,128)} all-to-all(f32[16,1,38400]{2,1,0:T(1,128)} %reshape.138), channel_id=1, replica_groups=mesh['lon'=16,'lat'=2] {'lon'}, dimensions={0} | all-to-all | bytes 4915200 | tf_op jit(solution)/shard_map/all_to_all | solution.py:65
  265.8 0.6 broadcast.118
  266.4 9.6 %reduce.6 = f32[16,38400]{1,0:T(8,128)} reduce(f32[16,1,38400]{2,1,0:T(1,128)} %all_to_all.36, f32[]{:T(128)} %broadcast.118), dimensions={1}, to_apply=%all_to_all.30.reduce_sub_computation | reduce | bytes 4915204 | tf_op jit(solution)/shard_map/all_to_all | solution.py:65
  276.0 16.8 %reshape.139 = f32[1280,6,2,40]{3,2,1,0:T(2,128)} reshape(f32[16,38400]{1,0:T(8,128)} %reduce.6) | data formatting | bytes 4915200
  292.8 10.2 %copy.42 = f32[2,6,40,16,80]{4,2,3,1,0:T(8,128)} copy(f32[2,6,40,16,80]{2,0,1,4,3:T(2,128)} %bitcast.81) | data formatting | bytes 4915200 | tf_op jit(solution)/shard_map/all_to_all | solution.py:65
  303.0 5.1 %copy.43 = f32[2,6,640,80]{2,3,1,0:T(8,128)} copy(f32[2,6,640,80]{3,2,1,0:T(8,128)} %bitcast.83) | data formatting | bytes 4915200 | tf_op jit(solution)/shard_map/all_to_all | solution.py:65
  308.1 4.1 %fusion.127 = (f32[2,6,80]{2,1,0:T(8,128)S(1)}, f32[2,6,80,640]{3,2,1,0:T(8,128)}) fusion(f32[2,6,80,640]{3,2,1,0:T(8,128)} %param.8, f32[2,6,640,80]{2,3,1,0:T(8,128)} %copy.43), kind=kLoop, calls=%fused_computation.203 | loop fusion | flops 1227840 | bytes 7376640 | tf_op jit(solution)/shard_map/reduce_sum | solution.py:68
  312.3 0.1 div.27
  312.3 2.2 multiply_reduce_fusion
  314.5 0.1 sqrt.12
  314.6 2.0 fusion.62
  316.6 0.0 copy-done
  316.6 16.0 %fusion.63 = f32[960,640]{1,0:T(8,128)} fusion(bf16[1280,640]{1,0:T(8,128)(2,1)S(1)} %copy-done, bf16[960,640]{1,0:T(8,128)(2,1)S(1)} %fusion.62, bf16[640,1280]{1,0:T(8,128)(2,1)} %param.10), kind=kOutput, calls=%fused_computation.130 | convolution fusion | flops 3225600000 | bytes 6963200 | tf_op jit(solution)/shard_map/dot_general | solution.py:73
  332.6 4.1 %add.109 = f32[2,6,80,640]{3,2,1,0:T(8,128)} add(f32[2,6,80,640]{3,2,1,0:T(8,128)} %get-tuple-element.30, f32[2,6,80,640]{3,2,1,0:T(8,128)} %bitcast.84) | non-fusion elementwise | flops 614400 | bytes 7372800 | tf_op jit(solution)/shard_map/add | solution.py:74
  (5 shorter events, 0.1 us)
Async XLA Ops:
  0.0 316.6 %copy-start = (bf16[1280,640]{1,0:T(8,128)(2,1)S(1)}, bf16[1280,640]{1,0:T(8,128)(2,1)}, u32[]{:S(2)}) copy-start(bf16[1280,640]{1,0:T(8,128)(2,1)} %param.11) | copy-start | bytes 4915204
  6.0 7.5 %copy-start.1 = (f32[2,7,640,40]{2,3,1,0:T(8,128)S(1)}, f32[2,7,640,40]{2,3,1,0:T(8,128)}, u32[]{:S(2)}) copy-start(f32[2,7,640,40]{2,3,1,0:T(8,128)} %param.9) | copy-start | bytes 4300804
  6.0 81.0 %all-to-all-start = ((f32[2,6,80,640]{2,0,1,3:T(2,128)}), f32[2,6,80,640]{2,0,1,3:T(2,128)}, u32[]{:S(2)}, u32[]{:S(2)}) async-start(f32[2,6,80,640]{2,0,1,3:T(2,128)} %copy.38), calls=%async_computation | async-start | bytes 7864320 | tf_op jit(solution)/shard_map/all_to_all | solution.py:39
  111.8 0.9 copy-start.2
  111.8 1.0 copy-start.3
  111.8 1.1 copy-start.4
  111.8 1.2 copy-start.5
  111.9 1.3 copy-start.6
  118.4 29.7 %collective-permute-start = (f32[2,3,40,1280]{3,2,1,0:T(8,128)S(1)}, f32[2,3,40,1280]{3,2,1,0:T(8,128)S(1)}, u32[]{:S(2)}, u32[]{:S(2)}) collective-permute-start(f32[2,3,40,1280]{3,2,1,0:T(8,128)S(1)} %get-tuple-element.32), channel_id=1, source_target_pairs={{0,1},{2,3},{4,5},{6,7},{8,9},{10,11},{12,13},{14,15},{16,17},{18,... | collective-permute-start | bytes 3686408 | tf_op jit(solution)/shard_map/ppermute | solution.py:10
  121.6 30.5 %collective-permute-start.1 = (f32[2,3,40,1280]{3,2,1,0:T(8,128)S(1)}, f32[2,3,40,1280]{3,2,1,0:T(8,128)S(1)}, u32[]{:S(2)}, u32[]{:S(2)}) collective-permute-start(f32[2,3,40,1280]{3,2,1,0:T(8,128)S(1)} %get-tuple-element.31), channel_id=1, source_target_pairs={{1,0},{3,2},{5,4},{7,6},{9,8},{11,10},{13,12},{15,14},{17,16},{19,... | collective-permute-start | bytes 3686408 | tf_op jit(solution)/shard_map/ppermute | solution.py:10
where the time goes:
time: 341 us; the launch traced here: 337 us
  local copies, waits for them, and re-layouts  77.6 us (23%)
  blocking collectives  75.2 us (22%)
  waiting for transfers between devices  72.3 us (21%)
  other arithmetic  57.4 us (17%)
  matrix products  41.9 us (12%)
  starting transfers between devices  12.2 us (4%)
    all_to_all x1, blocking collectives, body(): lax.all_to_all(grid_out, 'lon', split_axis=3, concat_axis=2, tiled=True)  75.2 us
    all_to_all x1, waiting for transfers between devices, body(): lax.all_to_all(field, 'lon', split_axis=3, concat_axis=2, tiled=True)  57.7 us
    unnamed x17, local copies, waits for them, and re-layouts  40.4 us
    dot_general x1, matrix products, body(): update = jnp.dot(hidden, w_out, preferred_element_type=jnp.float32)  16 us
    all_to_all x3, local copies, waits for them, and re-layouts, body(): lax.all_to_all(grid_out, 'lon', split_axis=3, concat_axis=2, tiled=True)  15.9 us
    ppermute x2, waiting for transfers between devices, shifted(): return lax.ppermute(block, axis, route)  14.5 us
    neg x1, other arithmetic, forward_table(): return jnp.concatenate([jnp.cos(angles), -jnp.sin(angles)], axis=1)  14.5 us
    dot_general x1, matrix products, body(): jnp.einsum('eilc,lk->eick', gridded, table_fwd, precision=lax.Precision.H...  14.5 us
  transfers between devices with their start and end apart: 3, of which 3 were waited for; matrix products, arithmetic and copies ran while one was open for 9% of the time, Pallas kernels for 0%

commit v1 on v0

v1 whole, which is shorter than its diff:
```python
import functools

import jax
import jax.numpy as jnp
import ml_dtypes
import numpy as np
from jax import lax
from jax.experimental import pallas as pl
from jax.experimental.pallas import tpu as pltpu
from jax.sharding import PartitionSpec as P

LANES = 128
HALO = 3
TAPS = 7
MESH = pl.DeviceIdType.MESH
F32 = jnp.float32
BF16 = jnp.bfloat16


def split_table(table):
    high = table.astype(ml_dtypes.bfloat16)
    low = (table - high.astype(np.float64)).astype(ml_dtypes.bfloat16)
    return high, low


def tables(length):
    modes = length // 2
    orders = np.arange(modes, dtype=np.int64)[:, None]
    places = np.arange(length, dtype=np.int64)[None, :]
    angles = 2.0 * np.pi / length * (orders * places % length).astype(np.float64)
    forward = np.concatenate([np.cos(angles), -np.sin(angles)], axis=0)
    weights = np.where(np.arange(modes) == 0, 1.0, 2.0) / length
    inverse = (forward * np.concatenate([weights, weights])[:, None]).T
    return split_table(forward) + split_table(np.ascontiguousarray(inverse))


def lane_index(rows):
    return lax.broadcasted_iota(jnp.int32, (rows, LANES), 1)


def rolled(block, shift):
    shift = shift % LANES
    return block if shift == 0 else pltpu.roll(block, shift, 1)


def split_value(value):
    high = value.astype(BF16)
    return high, (value - high.astype(F32)).astype(BF16)


def dot3(a_high, a_low, b_high, b_low):
    total = jnp.dot(a_high, b_high, preferred_element_type=F32)
    total += jnp.dot(a_low, b_high, preferred_element_type=F32)
    return total + jnp.dot(a_high, b_low, preferred_element_type=F32)


def kernel(
    groups, lats, field_hbm, filter_hbm, fwd_high_hbm, fwd_low_hbm, inv_high_hbm, inv_low_hbm, w_in_hbm, w_out_hbm,
    out_hbm, field, filt, fwd_high, fwd_low, inv_high, inv_low, w_in, w_out,
    packed, grid, grid_high, grid_low, spec, stack, coef, spec_high, spec_low, conv, back, mixed, normed, hidden, result,
    load_sem, send_sem, recv_sem, halo_send, halo_recv, home_send, home_recv, out_sem,
):
    members, rows_lat, lon_local, channels = field.shape
    width = channels // groups
    length = lon_local * groups
    modes = length // 2
    per_member = rows_lat // HALO
    chunks = members * per_member
    me = lax.axis_index("lon")
    lat = lax.axis_index("lat")
    own = pl.ds(pl.multiple_of(me * lon_local, 8), lon_local)
    has_low = lat > 0
    has_high = lat < lats - 1

    loads = [
        pltpu.make_async_copy(src, dst, load_sem.at[n])
        for n, (src, dst) in enumerate(
            [
                (field_hbm, field),
                (filter_hbm, filt),
                (fwd_high_hbm, fwd_high),
                (fwd_low_hbm, fwd_low),
                (inv_high_hbm, inv_high),
                (inv_low_hbm, inv_low),
                (w_in_hbm, w_in),
                (w_out_hbm, w_out),
            ]
        )
    ]
    for load in loads:
        load.start()

    barrier = pltpu.get_barrier_semaphore()

    def greet(d, carry):
        pl.semaphore_signal(barrier, inc=1, device_id=(lax.rem(me + d, groups), lat), device_id_type=MESH)
        return carry

    lax.fori_loop(1, groups, greet, 0)

    @pl.when(has_low)
    def _():
        pl.semaphore_signal(barrier, inc=1, device_id=(me, lat - 1), device_id_type=MESH)

    @pl.when(has_high)
    def _():
        pl.semaphore_signal(barrier, inc=1, device_id=(me, lat + 1), device_id_type=MESH)

    def pack(chunk):
        member, part = chunk // per_member, chunk % per_member
        lanes = lane_index(lon_local)
        for g in range(groups):
            total = jnp.zeros((lon_local, LANES), F32)
            for j in range(HALO):
                start = g * width
                for b in range(start // LANES, (start + width - 1) // LANES + 1):
                    first = max(start, b * LANES) - start
                    last = min(start + width, (b + 1) * LANES) - start
                    block = field[member, part * HALO + j, :, b * LANES : (b + 1) * LANES]
                    moved = rolled(block, j * width - (start - b * LANES))
                    keep = (lanes >= j * width + first) & (lanes < j * width + last)
                    total = jnp.where(keep, moved, total)
            packed[chunk, g] = total
        grid[chunk, own, :] = packed[chunk, me]

    def outward(chunk, d):
        peer = lax.rem(me + d, groups)
        return pltpu.make_async_remote_copy(
            src_ref=packed.at[chunk, peer],
            dst_ref=grid.at[chunk, own],
            send_sem=send_sem.at[chunk, d],
            recv_sem=recv_sem.at[chunk, d],
            device_id=(peer, lat),
            device_id_type=MESH,
        )

    def homeward(chunk, d):
        peer = lax.rem(me + d, groups)
        return pltpu.make_async_remote_copy(
            src_ref=conv.at[chunk, pl.ds(pl.multiple_of(peer * lon_local, 8), lon_local)],
            dst_ref=back.at[chunk, me],
            send_sem=home_send.at[chunk, d],
            recv_sem=home_recv.at[chunk, d],
            device_id=(peer, lat),
            device_id_type=MESH,
        )

    def each(action):
        def step(d, carry):
            action(d)
            return carry

        lax.fori_loop(1, groups, step, 0)

    def halo_up(member):
        return pltpu.make_async_remote_copy(
            src_ref=spec.at[member, per_member],
            dst_ref=spec.at[member, 0],
            send_sem=halo_send.at[member, 0],
            recv_sem=halo_recv.at[member, 0],
            device_id=(me, lat + 1),
            device_id_type=MESH,
        )

    def halo_down(member):
        return pltpu.make_async_remote_copy(
            src_ref=spec.at[member, 1],
            dst_ref=spec.at[member, per_member + 1],
            send_sem=halo_send.at[member, 1],
            recv_sem=halo_recv.at[member, 1],
            device_id=(me, lat - 1),
            device_id_type=MESH,
        )

    loads[0].wait()
    pack(0)
    others = groups - 1 + has_low.astype(jnp.int32) + has_high.astype(jnp.int32)
    pl.semaphore_wait(barrier, others)
    each(lambda d: outward(0, d).start())

    def pack_and_send(chunk, carry):
        pack(chunk)
        each(lambda d: outward(chunk, d).start())
        return carry

    lax.fori_loop(1, chunks, pack_and_send, 0)

    @pl.when(jnp.logical_not(has_low))
    def _():
        for member in range(members):
            spec[member, 0] = jnp.zeros((length, LANES), F32)

    @pl.when(jnp.logical_not(has_high))
    def _():
        for member in range(members):
            spec[member, per_member + 1] = jnp.zeros((length, LANES), F32)

    stack[...] = jnp.zeros_like(stack)
    loads[1].wait()

    def spread(n, carry):
        part = filt[n // TAPS, n % TAPS]
        for j in range(HALO):
            stack[j * width : (j + 1) * width, :] = part
        coef[n // TAPS, n % TAPS] = stack[...].T
        return carry

    lax.fori_loop(0, 2 * TAPS, spread, 0)
    for load in loads[2:]:
        load.wait()

    tile = 256
    columns = per_member * LANES

    def transform(member):
        for part in range(per_member):
            chunk = member * per_member + part
            each(lambda d: outward(chunk, d).wait_recv())

            def halve(t, carry):
                rows = pl.ds(pl.multiple_of(t * tile, tile), tile)
                high, low = split_value(grid[chunk, rows, :])
                grid_high[rows, part * LANES : (part + 1) * LANES] = high
                grid_low[rows, part * LANES : (part + 1) * LANES] = low
                return carry

            lax.fori_loop(0, length // tile, halve, 0)

        def step(t, carry):
            rows = pl.ds(pl.multiple_of(t * tile, tile), tile)
            value = dot3(fwd_high[rows, :], fwd_low[rows, :], grid_high[...], grid_low[...])
            for part in range(per_member):
                spec[member, part + 1, rows, :] = value[:, part * LANES : (part + 1) * LANES]
            return carry

        lax.fori_loop(0, length // tile, step, 0)

        @pl.when(has_high)
        def _():
            halo_up(member).start()

        @pl.when(has_low)
        def _():
            halo_down(member).start()

    def filtered(member):
        @pl.when(has_low)
        def _():
            halo_up(member).wait_recv()

        @pl.when(has_high)
        def _():
            halo_down(member).wait_recv()

        step_rows = 16
        lanes = lane_index(step_rows)

        def step(t, carry):
            at = pl.multiple_of(t * step_rows, step_rows)
            real_rows = pl.ds(at, step_rows)
            imag_rows = pl.ds(modes + at, step_rows)
            real = [spec[member, p, real_rows, :] for p in range(per_member + 2)]
            imag = [spec[member, p, imag_rows, :] for p in range(per_member + 2)]

            def at_shift(values, p, s):
                if s % HALO == 0:
                    return values[p + s // HALO]
                if s > 0:
                    here, there, cut = values[p], values[p + 1], (HALO - s) * width
                    return jnp.where(lanes < cut, rolled(here, -s * width), rolled(there, cut))
                here, there, cut = values[p], values[p - 1], -s * width
                return jnp.where(lanes < cut, rolled(there, -(HALO + s) * width), rolled(here, cut))

            for part in range(per_member):
                total_real = jnp.zeros((step_rows, LANES), F32)
                total_imag = jnp.zeros((step_rows, LANES), F32)
                for d in range(TAPS):
                    h_real = coef[0, d, real_rows, :]
                    h_imag = coef[1, d, real_rows, :]
                    x_real = at_shift(real, part + 1, d - HALO)
                    x_imag = at_shift(imag, part + 1, d - HALO)
                    total_real += h_real * x_real - h_imag * x_imag
                    total_imag += h_real * x_imag + h_imag * x_real
                side = slice(part * LANES, (part + 1) * LANES)
                high, low = split_value(total_real)
                spec_high[real_rows, side] = high
                spec_low[real_rows, side] = low
                high, low = split_value(total_imag)
                spec_high[imag_rows, side] = high
                spec_low[imag_rows, side] = low
            return carry

        lax.fori_loop(0, modes // step_rows, step, 0)

    def inverse(member):
        def step(t, carry):
            rows = pl.ds(pl.multiple_of(t * tile, tile), tile)
            value = dot3(inv_high[rows, :], inv_low[rows, :], spec_high[...], spec_low[...])
            for part in range(per_member):
                conv[member * per_member + part, rows, :] = value[:, part * LANES : (part + 1) * LANES]
            return carry

        lax.fori_loop(0, length // tile, step, 0)
        for part in range(per_member):
            chunk = member * per_member + part
            each(lambda d: homeward(chunk, d).start())
            back[chunk, me] = conv[chunk, own, :]

    def finish(chunk):
        member, part = chunk // per_member, chunk % per_member
        each(lambda d: homeward(chunk, d).wait_recv())
        lanes = lane_index(lon_local)
        for j in range(HALO):
            for b in range(channels // LANES):
                total = jnp.zeros((lon_local, LANES), F32)
                for g in range(b * LANES // width, ((b + 1) * LANES - 1) // width + 1):
                    start = g * width - b * LANES
                    moved = rolled(back[chunk, g], start - j * width)
                    keep = (lanes >= start) & (lanes < start + width)
                    total = jnp.where(keep, moved, total)
                side = slice(b * LANES, (b + 1) * LANES)
                mixed[j * lon_local : (j + 1) * lon_local, side] = field[member, part * HALO + j, :, side] + total
        rows = mixed[...]
        center = jnp.mean(rows, axis=1, keepdims=True)
        away = rows - center
        variance = jnp.mean(away * away, axis=1, keepdims=True)
        normed[...] = (away / jnp.sqrt(variance + 1e-05)).astype(BF16)
        hidden_units = hidden.shape[1]
        for q in range(hidden_units // 256):
            side = slice(q * 256, (q + 1) * 256)
            before = jnp.dot(normed[...], w_in[:, side], preferred_element_type=F32)
            value = 0.5 * before * (1.0 + lax.erf(before * np.float32(np.sqrt(0.5))))
            hidden[:, side] = value.astype(BF16)
        for b in range(channels // LANES):
            side = slice(b * LANES, (b + 1) * LANES)
            update = jnp.dot(hidden[...], w_out[:, side], preferred_element_type=F32) + mixed[:, side]
            for j in range(HALO):
                result[member, part * HALO + j, :, side] = update[j * lon_local : (j + 1) * lon_local]
        saved(chunk).start()

    def saved(chunk):
        member, part = chunk // per_member, chunk % per_member
        place = pl.ds(part * HALO, HALO)
        return pltpu.make_async_copy(result.at[member, place], out_hbm.at[member, place], out_sem.at[chunk])

    for member in range(members):
        transform(member)
        filtered(member)
        inverse(member)

    def last(chunk, carry):
        finish(chunk)
        return carry

    lax.fori_loop(0, chunks, last, 0)

    def close(chunk, carry):
        saved(chunk).wait()
        each(lambda d: outward(chunk, d).wait_send())
        each(lambda d: homeward(chunk, d).wait_send())
        return carry

    lax.fori_loop(0, chunks, close, 0)
    for member in range(members):

        @pl.when(has_high)
        def _():
            halo_up(member).wait_send()

        @pl.when(has_low)
        def _():
            halo_down(member).wait_send()


def body(groups, lats, field, spectral_filter, w_in, w_out, fwd_high, fwd_low, inv_high, inv_low):
    members, rows_lat, lon_local, channels = field.shape
    hidden_units = w_in.shape[1]
    length = lon_local * groups
    modes = length // 2
    width = channels // groups
    per_member = rows_lat // HALO
    chunks = members * per_member
    columns = per_member * LANES
    filt = jnp.transpose(spectral_filter, (0, 1, 3, 2))
    dma = pltpu.SemaphoreType.DMA
    return pl.pallas_call(
        functools.partial(kernel, groups, lats),
        out_shape=jax.ShapeDtypeStruct(field.shape, F32),
        in_specs=[pl.BlockSpec(memory_space=pl.ANY)] * 8,
        out_specs=pl.BlockSpec(memory_space=pl.ANY),
        scratch_shapes=[
            pltpu.VMEM(field.shape, F32),
            pltpu.VMEM((2, TAPS, width, modes), F32),
            pltpu.VMEM((length, length), BF16),
            pltpu.VMEM((length, length), BF16),
            pltpu.VMEM((length, length), BF16),
            pltpu.VMEM((length, length), BF16),
            pltpu.VMEM(w_in.shape, BF16),
            pltpu.VMEM(w_out.shape, BF16),
            pltpu.VMEM((chunks, groups, lon_local, LANES), F32),
            pltpu.VMEM((chunks, length, LANES), F32),
            pltpu.VMEM((length, columns), BF16),
            pltpu.VMEM((length, columns), BF16),
            pltpu.VMEM((members, per_member + 2, length, LANES), F32),
            pltpu.VMEM((LANES, modes), F32),
            pltpu.VMEM((2, TAPS, modes, LANES), F32),
            pltpu.VMEM((length, columns), BF16),
            pltpu.VMEM((length, columns), BF16),
            pltpu.VMEM((chunks, length, LANES), F32),
            pltpu.VMEM((chunks, groups, lon_local, LANES), F32),
            pltpu.VMEM((HALO * lon_local, channels), F32),
            pltpu.VMEM((HALO * lon_local, channels), BF16),
            pltpu.VMEM((HALO * lon_local, hidden_units), BF16),
            pltpu.VMEM(field.shape, F32),
            dma((8,)),
            dma((chunks, groups)),
            dma((chunks, groups)),
            dma((members, 2)),
            dma((members, 2)),
            dma((chunks, groups)),
            dma((chunks, groups)),
            dma((chunks,)),
        ],
        compiler_params=pltpu.CompilerParams(
            collective_id=0, has_side_effects=True, vmem_limit_bytes=60 * 2**20
        ),
    )(field, filt, fwd_high, fwd_low, inv_high, inv_low, w_in, w_out)


def solution(mesh):
    groups, lats = mesh.shape["lon"], mesh.shape["lat"]
    in_specs = (P(None, "lat", "lon", None), P(None, None, None, "lon"), P(), P(), P(), P(), P(), P())
    out_specs = P(None, "lat", "lon", None)
    mapped = jax.shard_map(
        functools.partial(body, groups, lats), mesh=mesh, in_specs=in_specs, out_specs=out_specs, check_vma=False
    )

    def run(field, spectral_filter, w_in, w_out):
        return mapped(field, spectral_filter, w_in, w_out, *tables(field.shape[2]))

    return run
```

time: 341 us -> 137 us (0.40)
  the two profiles are of different devices: /device:TPU:1 before, /device:TPU:29 now
where the time goes in v1:
time: 137 us
  Pallas kernels  134 us (98%)
  local copies, waits for them, and re-layouts  3.29 us (2%)
    pallas_call x1, Pallas kernels, body(): pl.pallas_call(functools.partial(kernel, groups, lats), out_shape=jax.Sha...  134 us
    unnamed x1, local copies, waits for them, and re-layouts  3.29 us

profile of v1, /device:TPU:29, one launch (start us, length us, event | category | flops | bytes accessed | tf_op | source)
XLA Modules:
  0.0 137.0 jit_solution(6723593905859917407)
XLA Ops:
  0.0 133.7 %shard_map.82 = f32[2,6,80,640]{3,2,1,0:T(8,128)} custom-call(f32[2,6,80,640]{3,2,1,0:T(8,128)} %field_hbm.1, f32[2,7,40,640]{3,2,1,0:T(8,128)} %bitcast.1, bf16[1280,1280]{1,0:T(8,128)(2,1)} %constant.8.clone.fwd_high_hbm, bf16[1280,1280]{1,0:T(8,128)(2,1)} %constant.9.clone.fwd_low_hbm, bf16[1280,1280]{1,0:T(8,128)(2,1)} %constant.10.clone.inv_high_hbm, ...), custom_call_target="tpu_custom_call" | custom-call | tf_op jit(solution)/shard_map/pallas_call | solution.py:386
  133.7 3.3 %copy.10 = f32[2,6,80,640]{3,2,1,0:T(8,128)} copy(f32[2,6,80,640]{3,2,1,0:T(8,128)} %shard_map.82) | data formatting | bytes 4915200
